TPU v7x, 256 devices: a whole 4x4x8 slice. The times are simulated.
256 devices in a mesh: dp: 32 (over x, z), tensor: 8 (over y, core).
Axes of the slice: x: 4, y: 4, z: 8, core: 2. Of those that a mesh axis runs over, the one named last changes fastest.
Arguments:
- gate_input: bfloat16 [8192, 14336], P('dp', 'tensor'), may hold values from -12 to 12
- up_input: bfloat16 [8192, 14336], P('dp', 'tensor'), may hold values from -12 to 12
- grad_out: bfloat16 [8192, 4096], P('dp'), may hold values from -0.0501 to 0.0501
Outputs:
- combined: bfloat16 [14336, 4096], P('tensor', 'dp')
All inputs are finite; a program needn't handle non-finite values.
Results may differ from a plain program's by a relative error of at most 0.0059.
Values may be sent and summed in bfloat16 or wider, within the bound.
A program may use at most 128 MiB of HBM per device.

v0:
```python
import jax
import jax.numpy as jnp
from jax import lax
from jax.sharding import PartitionSpec as P

epsilon = 1e-06


def partner(block, axis, distance):
    count = lax.axis_size(axis)
    route = []
    for low in range(count):
        high = low | 1 << distance
        if high != low and high < count:
            route += [(low, high), (high, low)]
    return lax.ppermute(block, axis, route)


def outer_grad(hidden, grad_cols):
    product = lax.dot_general(
        hidden, grad_cols, (((0,), (0,)), ((), ())), preferred_element_type=jnp.float32
    )
    return product.astype(jnp.bfloat16)


def group_totals(partials, section_bit, levels):
    for pair_bit in range(section_bit, levels):
        partials = partials + partner(partials, "dp", pair_bit)
    return lax.psum(partials, "tensor")


def combine_section(kept_part, received, upper_half, section_bit, levels):
    kept_f = kept_part.astype(jnp.float32)
    recv_f = received.astype(jnp.float32)
    self_kept = jnp.sum(kept_f * kept_f)
    self_recv = jnp.sum(recv_f * recv_f)
    cross_term = jnp.sum(kept_f * recv_f)
    lower = upper_half == 0
    partials = jnp.stack(
        [jnp.where(lower, self_kept, self_recv), jnp.where(lower, self_recv, self_kept), cross_term]
    )
    totals = group_totals(partials, section_bit, levels)
    coef_first = 1.0 - totals[2] / (2.0 * (totals[0] + epsilon))
    coef_second = 1.0 - totals[2] / (2.0 * (totals[1] + epsilon))
    coef_kept = jnp.where(lower, coef_first, coef_second)
    coef_recv = jnp.where(lower, coef_second, coef_first)
    merged = coef_kept * kept_f + coef_recv * recv_f
    return merged.astype(jnp.bfloat16)


def body(gate_input, up_input, grad_out):
    hidden = (jax.nn.silu(gate_input.astype(jnp.float32)) * up_input.astype(jnp.float32)).astype(
        jnp.bfloat16
    )
    levels = lax.axis_size("dp").bit_length() - 1
    rank_dp = lax.axis_index("dp")
    col_width = grad_out.shape[1]
    top_bit = levels - 1
    half_cols = col_width // 2
    upper_half = rank_dp >> top_bit & 1
    own_cols = lax.dynamic_slice_in_dim(grad_out, upper_half * half_cols, half_cols, 1)
    give_cols = lax.dynamic_slice_in_dim(grad_out, (1 - upper_half) * half_cols, half_cols, 1)
    kept_part = outer_grad(hidden, own_cols)
    sent_part = outer_grad(hidden, give_cols)
    received = partner(sent_part, "dp", top_bit)
    current = combine_section(kept_part, received, upper_half, top_bit, levels)
    for section_bit in range(top_bit - 1, -1, -1):
        half_cols = current.shape[1] // 2
        upper_half = rank_dp >> section_bit & 1
        kept_part = lax.dynamic_slice_in_dim(current, upper_half * half_cols, half_cols, 1)
        sent_part = lax.dynamic_slice_in_dim(current, (1 - upper_half) * half_cols, half_cols, 1)
        received = partner(sent_part, "dp", section_bit)
        current = combine_section(kept_part, received, upper_half, section_bit, levels)
    return current


def solution(mesh):
    placed = (P("dp", "tensor"), P("dp", "tensor"), P("dp", None))
    return jax.shard_map(
        body, mesh=mesh, in_specs=placed, out_specs=P("tensor", "dp"), check_vma=False
    )
```

profile of v0, /device:TPU:1, one launch (start us, length us, event | category | flops | bytes accessed | tf_op | source)
XLA Modules:
  0.0 626.1 jit_solution(17620896217234530345)
XLA Ops:
  0.0 1.6 copy-done
  1.6 6.8 %convolution_convert_fusion = bf16[1792,2048]{1,0:T(8,128)(2,1)} fusion(bf16[256,4096]{1,0:T(8,128)(2,1)S(1)} %copy-done, s32[]{:T(128)S(6)} %select_n.92, bf16[256,1792]{1,0:T(8,128)(2,1)} %param.4, bf16[256,1792]{1,0:T(8,128)(2,1)} %param.3), kind=kOutput, calls=%fused_computation.15 | convolution fusion | flops 1886388224 | bytes 10223620 | tf_op jit(solution)/shard_map/dot_general | solution.py:20
  8.4 3.6 collective-permute-start
  12.0 157.0 %collective-permute-done = bf16[1792,2048]{1,0:T(8,128)(2,1)} collective-permute-done((bf16[1792,2048]{1,0:T(8,128)(2,1)}, bf16[1792,2048]{1,0:T(8,128)(2,1)}, u32[]{:S(2)}, u32[]{:S(2)}) %collective-permute-start) | collective-permute-done | bytes 7340064 | tf_op jit(solution)/shard_map/ppermute | solution.py:16
  169.0 11.6 %fusion = (f32[]{:T(128)}, f32[]{:T(128)}, f32[]{:T(128)}, bf16[1792,2048]{1,0:T(8,128)(2,1)}) fusion(bf16[1792,2048]{1,0:T(8,128)(2,1)} %collective-permute-done, bf16[256,4096]{1,0:T(8,128)(2,1)S(1)} %copy-done, s32[]{:T(128)S(6)} %select_n.91, bf16[256,1792]{1,0:T(8,128)(2,1)S(1)} %copy-done.4, bf16[256,1792]{1,0:T(8,128)(2,1)} %param.3), kind=kOutput, calls=%fused_computation.5 | convolution fusion | flops 1915748352 | bytes 17563664 | tf_op jit(solution)/shard_map/dot_general | solution.py:20
  182.9 0.8 pad_maximum_fusion
  183.7 3.7 collective-permute-start.1
  187.4 0.9 collective-permute-done.1
  188.4 0.8 fusion.45
  189.1 14.9 %psum.35 = f32[3]{0:T(128)S(1)} all-reduce(f32[3]{0:T(128)S(1)} %fusion.45), channel_id=1, replica_groups=mesh['dp'=32,'tensor'=8] {'tensor'}, use_global_device_ids=true, to_apply=%region_3.4 | all-reduce | flops 3 | bytes 24 | tf_op jit(solution)/shard_map/psum | solution.py:29
  207.2 12.7 %fusion.2 = bf16[1792,2048]{1,0:T(8,128)(2,1)} fusion(bf16[1792,2048]{1,0:T(8,128)(2,1)} %get-tuple-element.35, bf16[1792,2048]{1,0:T(8,128)(2,1)} %collective-permute-done, f32[]{:T(128)S(6)} %select_n.96, f32[]{:T(128)S(6)} %select_n.95), kind=kLoop, calls=%fused_computation.7 | loop fusion | flops 22020096 | bytes 22020104 | tf_op jit(solution)/shard_map/convert_element_type | solution.py:48
  219.9 4.3 constant_dynamic-slice_fusion.3
  224.2 1.2 collective-permute-start.2
  225.4 79.1 %collective-permute-done.2 = bf16[1792,1024]{1,0:T(8,128)(2,1)} collective-permute-done((bf16[1792,1024]{1,0:T(8,128)(2,1)}, bf16[1792,1024]{1,0:T(8,128)(2,1)}, u32[]{:S(2)}, u32[]{:S(2)}) %collective-permute-start.2) | collective-permute-done | bytes 3670048 | tf_op jit(solution)/shard_map/ppermute | solution.py:16
  304.5 4.7 fusion.5
  312.3 1.2 collective-permute-start.3
  313.6 1.2 collective-permute-done.3
  315.4 2.8 collective-permute-start.4
  318.1 1.2 collective-permute-done.4
  319.9 15.8 %psum.36 = f32[3]{0:T(128)S(1)} all-reduce(f32[3]{0:T(128)S(1)} %fusion.49), channel_id=1, replica_groups=mesh['dp'=32,'tensor'=8] {'tensor'}, use_global_device_ids=true, to_apply=%region_7.8 | all-reduce | flops 3 | bytes 24 | tf_op jit(solution)/shard_map/psum | solution.py:29
  338.8 5.0 fusion.7
  343.9 1.8 copy-done.1
  345.7 1.5 constant_dynamic-slice_fusion.2
  347.2 6.9 %collective-permute-start.5 = (bf16[1792,512]{1,0:T(8,128)(2,1)}, bf16[1792,512]{1,0:T(8,128)(2,1)}, u32[]{:S(2)}, u32[]{:S(2)}) collective-permute-start(bf16[1792,512]{1,0:T(8,128)(2,1)} %constant_dynamic-slice_fusion.2), channel_id=1, source_target_pairs={{0,32},{32,0},{8,40},{40,8},{16,48},{48,16},{24,56},{56,24},{64,96... | collective-permute-start | bytes 5505032 | tf_op jit(solution)/shard_map/ppermute | solution.py:16
  354.1 52.4 %collective-permute-done.5 = bf16[1792,512]{1,0:T(8,128)(2,1)} collective-permute-done((bf16[1792,512]{1,0:T(8,128)(2,1)}, bf16[1792,512]{1,0:T(8,128)(2,1)}, u32[]{:S(2)}, u32[]{:S(2)}) %collective-permute-start.5) | collective-permute-done | bytes 1835040 | tf_op jit(solution)/shard_map/ppermute | solution.py:16
  406.5 3.7 fusion.10
  413.4 5.5 collective-permute-start.6
  418.9 1.0 collective-permute-done.6
  420.5 1.4 collective-permute-start.7
  421.9 1.0 collective-permute-done.7
  423.6 2.9 collective-permute-start.8
  426.5 1.0 collective-permute-done.8
  427.5 42.7 %psum.37 = f32[3]{0:T(128)S(1)} all-reduce(f32[3]{0:T(128)S(1)} %add.162), channel_id=1, replica_groups=mesh['dp'=32,'tensor'=8] {'tensor'}, use_global_device_ids=true, to_apply=%region_11.12 | all-reduce | flops 3 | bytes 24 | tf_op jit(solution)/shard_map/psum | solution.py:29
  473.4 2.7 fusion.12
  476.1 1.2 copy-done.2
  477.4 1.0 constant_dynamic-slice_fusion.1
  478.4 2.1 collective-permute-start.9
  480.4 39.9 %collective-permute-done.9 = bf16[1792,256]{1,0:T(8,128)(2,1)S(1)} collective-permute-done((bf16[1792,256]{1,0:T(8,128)(2,1)}, bf16[1792,256]{1,0:T(8,128)(2,1)S(1)}, u32[]{:S(2)}, u32[]{:S(2)}) %collective-permute-start.9) | collective-permute-done | bytes 917536 | tf_op jit(solution)/shard_map/ppermute | solution.py:16
  520.4 2.7 fusion.19
  526.3 3.3 collective-permute-done.10
  530.3 5.7 collective-permute-start.11
  536.0 0.9 collective-permute-done.11
  537.7 1.3 collective-permute-start.12
  539.0 1.1 collective-permute-done.12
  540.1 2.7 collective-permute-start.13
  542.9 1.2 collective-permute-done.13
  544.0 17.5 %psum.38 = f32[3]{0:T(128)S(1)} all-reduce(f32[3]{0:T(128)S(1)} %add.171), channel_id=1, replica_groups=mesh['dp'=32,'tensor'=8] {'tensor'}, use_global_device_ids=true, to_apply=%region_15.16 | all-reduce | flops 3 | bytes 24 | tf_op jit(solution)/shard_map/psum | solution.py:29
  564.7 1.8 fusion.21
  566.5 0.8 constant_dynamic-slice_fusion
  567.3 11.6 %collective-permute-done.14 = bf16[1792,128]{1,0:T(8,128)(2,1)S(1)} collective-permute-done((bf16[1792,128]{1,0:T(8,128)(2,1)}, bf16[1792,128]{1,0:T(8,128)(2,1)S(1)}, u32[]{:S(2)}, u32[]{:S(2)}) %collective-permute-start.14) | collective-permute-done | bytes 458784 | tf_op jit(solution)/shard_map/ppermute | solution.py:16
  579.0 0.9 fusion.27
  582.3 0.8 pad_maximum_fusion.4
  583.4 2.1 collective-permute-done.15
  585.5 0.8 fusion.41
  586.9 2.7 collective-permute-done.16
  589.6 0.8 fusion.46
  590.4 5.7 collective-permute-start.17
  596.0 0.9 collective-permute-done.17
  597.0 1.2 collective-permute-start.18
  598.2 1.2 collective-permute-done.18
  599.4 2.7 collective-permute-start.19
  602.1 1.1 collective-permute-done.19
  603.3 18.7 %psum.39 = f32[3]{0:T(128)S(1)} all-reduce(f32[3]{0:T(128)S(1)} %add.181), channel_id=1, replica_groups=mesh['dp'=32,'tensor'=8] {'tensor'}, use_global_device_ids=true, to_apply=%region_19.20 | all-reduce | flops 3 | bytes 24 | tf_op jit(solution)/shard_map/psum | solution.py:29
  625.1 1.0 fusion.29
  (31 shorter events, 10.2 us)
Async XLA Ops:
  0.0 1.6 copy-start
  1.6 167.4 %copy-start.4 = (bf16[256,1792]{1,0:T(8,128)(2,1)S(1)}, bf16[256,1792]{1,0:T(8,128)(2,1)}, u32[]{:S(2)}) copy-start(bf16[256,1792]{1,0:T(8,128)(2,1)} %param.4) | copy-start | bytes 2752516
  8.4 160.5 %collective-permute-start = (bf16[1792,2048]{1,0:T(8,128)(2,1)}, bf16[1792,2048]{1,0:T(8,128)(2,1)}, u32[]{:S(2)}, u32[]{:S(2)}) collective-permute-start(bf16[1792,2048]{1,0:T(8,128)(2,1)} %convolution_convert_fusion), channel_id=1, source_target_pairs={{0,128},{128,0},{8,136},{136,8},{16,144},{144,16},{24,152},{152,24... | collective-permute-start | bytes 22020104 | tf_op jit(solution)/shard_map/ppermute | solution.py:16
  183.7 4.7 collective-permute-start.1
  224.2 80.3 %collective-permute-start.2 = (bf16[1792,1024]{1,0:T(8,128)(2,1)}, bf16[1792,1024]{1,0:T(8,128)(2,1)}, u32[]{:S(2)}, u32[]{:S(2)}) collective-permute-start(bf16[1792,1024]{1,0:T(8,128)(2,1)} %constant_dynamic-slice_fusion.3), channel_id=1, source_target_pairs={{0,64},{64,0},{8,72},{72,8},{16,80},{80,16},{24,88},{88,24},{32,96... | collective-permute-start | bytes 11010056 | tf_op jit(solution)/shard_map/ppermute | solution.py:16
  312.3 2.4 collective-permute-start.3
  315.4 3.9 collective-permute-start.4
  343.9 1.8 copy-start.1
  347.2 59.3 %collective-permute-start.5 = (bf16[1792,512]{1,0:T(8,128)(2,1)}, bf16[1792,512]{1,0:T(8,128)(2,1)}, u32[]{:S(2)}, u32[]{:S(2)}) collective-permute-start(bf16[1792,512]{1,0:T(8,128)(2,1)} %constant_dynamic-slice_fusion.2), channel_id=1, source_target_pairs={{0,32},{32,0},{8,40},{40,8},{16,48},{48,16},{24,56},{56,24},{64,96... | collective-permute-start | bytes 5505032 | tf_op jit(solution)/shard_map/ppermute | solution.py:16
  413.4 6.5 %collective-permute-start.6 = (f32[3]{0:T(128)S(1)}, f32[3]{0:T(128)S(1)}, u32[]{:S(2)}, u32[]{:S(2)}) collective-permute-start(f32[3]{0:T(128)S(1)} %pad_maximum_fusion.2), channel_id=1, source_target_pairs={{0,32},{32,0},{8,40},{40,8},{16,48},{48,16},{24,56},{56,24},{64,96... | collective-permute-start | bytes 44 | tf_op jit(solution)/shard_map/ppermute | solution.py:16
  420.5 2.4 collective-permute-start.7
  423.6 3.9 collective-permute-start.8
  476.1 1.3 copy-start.2
  478.4 42.0 %collective-permute-start.9 = (bf16[1792,256]{1,0:T(8,128)(2,1)}, bf16[1792,256]{1,0:T(8,128)(2,1)S(1)}, u32[]{:S(2)}, u32[]{:S(2)}) collective-permute-start(bf16[1792,256]{1,0:T(8,128)(2,1)} %constant_dynamic-slice_fusion.1), channel_id=1, source_target_pairs={{0,16},{16,0},{8,24},{24,8},{32,48},{48,32},{40,56},{56,40},{64,80... | collective-permute-start | bytes 2752520 | tf_op jit(solution)/shard_map/ppermute | solution.py:16
  520.4 44.3 %copy-start.3 = (bf16[1792,256]{1,0:T(8,128)(2,1)}, bf16[1792,256]{1,0:T(8,128)(2,1)S(1)}, u32[]{:S(2)}) copy-start(bf16[1792,256]{1,0:T(8,128)(2,1)S(1)} %collective-permute-done.9) | copy-start | bytes 2752516
  526.2 3.3 collective-permute-start.10
  530.3 6.7 %collective-permute-start.11 = (f32[3]{0:T(128)S(1)}, f32[3]{0:T(128)S(1)}, u32[]{:S(2)}, u32[]{:S(2)}) collective-permute-start(f32[3]{0:T(128)S(1)} %fusion.42), channel_id=1, source_target_pairs={{0,32},{32,0},{8,40},{40,8},{16,48},{48,16},{24,56},{56,24},{64,96... | collective-permute-start | bytes 44 | tf_op jit(solution)/shard_map/ppermute | solution.py:16
  537.7 2.4 collective-permute-start.12
  540.1 3.9 collective-permute-start.13
  567.3 11.6 %collective-permute-start.14 = (bf16[1792,128]{1,0:T(8,128)(2,1)}, bf16[1792,128]{1,0:T(8,128)(2,1)S(1)}, u32[]{:S(2)}, u32[]{:S(2)}) collective-permute-start(bf16[1792,128]{1,0:T(8,128)(2,1)} %constant_dynamic-slice_fusion), channel_id=1, source_target_pairs={{0,8},{8,0},{16,24},{24,16},{32,40},{40,32},{48,56},{56,48},{64,72... | collective-permute-start | bytes 1376264 | tf_op jit(solution)/shard_map/ppermute | solution.py:16
  583.1 2.4 collective-permute-start.15
  586.3 3.3 collective-permute-start.16
  590.4 6.6 %collective-permute-start.17 = (f32[3]{0:T(128)S(1)}, f32[3]{0:T(128)S(1)}, u32[]{:S(2)}, u32[]{:S(2)}) collective-permute-start(f32[3]{0:T(128)S(1)} %fusion.46), channel_id=1, source_target_pairs={{0,32},{32,0},{8,40},{40,8},{16,48},{48,16},{24,56},{56,24},{64,96... | collective-permute-start | bytes 44 | tf_op jit(solution)/shard_map/ppermute | solution.py:16
  597.0 2.4 collective-permute-start.18
  599.4 3.9 collective-permute-start.19
where the time goes:
time: 627 us; the launch traced here: 626 us
  waiting for transfers between devices  361 us (58%)
  blocking collectives  110 us (18%)
  starting transfers between devices  51.7 us (8%)
  other arithmetic  45 us (7%)
  between operations  25 us (4%)
  matrix products  18.4 us (3%)
  local copies, waits for them, and re-layouts  15.5 us (2%)
    ppermute x20, waiting for transfers between devices, partner(): return lax.ppermute(block, axis, route)  361 us
    psum x5, blocking collectives, group_totals(): return lax.psum(partials, 'tensor')  110 us
    ppermute x20, starting transfers between devices, partner(): return lax.ppermute(block, axis, route)  51.7 us
    convert_element_type x5, other arithmetic, combine_section(): return merged.astype(jnp.bfloat16)  23.2 us
    dot_general x2, matrix products, outer_grad(): lax.dot_general(hidden, grad_cols, (((0,), (0,)), ((), ())), preferred_el...  18.4 us
  transfers between devices with their start and end apart: 20, of which 20 were waited for; matrix products, arithmetic and copies ran while one was open for 0% of the time, Pallas kernels for 0%

commit v1 on v0

v1 whole, which is shorter than its diff:
```python
import jax
import jax.numpy as jnp
from jax import lax
from jax.experimental import pallas as pl
from jax.experimental.pallas import tpu as pltpu
from jax.sharding import PartitionSpec as P

epsilon = 1e-06
MESH = pl.DeviceIdType.MESH
NX, NZ, NT = 4, 8, 8
TOK = 256
HID = 1792
MB = HID // NZ
NB = 1024
TR = TOK // NT
ORDER = (0, 7, 1, 6, 2, 5, 3, 4)
PAIRS4 = [(i, j) for i in range(4) for j in range(i, 4)]
PAIRS8 = [(i, j) for i in range(8) for j in range(i, 8)]


def pair_coefs(aa, bb, ab):
    aa = jnp.maximum(aa, 0.0)
    bb = jnp.maximum(bb, 0.0)
    bound = jnp.sqrt(aa) * jnp.sqrt(bb)
    ab = jnp.clip(ab, -bound, bound)
    return 1.0 - ab / (2.0 * (aa + epsilon)), 1.0 - ab / (2.0 * (bb + epsilon))


def tree_weights(gram, count):
    def get(table, i, j):
        return table[(min(i, j), max(i, j))]

    weights = [None] * count
    while count > 1:
        half = count // 2
        coefs = [
            pair_coefs(gram[(j, j)], gram[(j + half, j + half)], get(gram, j, j + half))
            for j in range(half)
        ]
        merged = {}
        for i in range(half):
            for j in range(i, half):
                merged[(i, j)] = (
                    coefs[i][0] * coefs[j][0] * get(gram, i, j)
                    + coefs[i][0] * coefs[j][1] * get(gram, i, j + half)
                    + coefs[i][1] * coefs[j][0] * get(gram, i + half, j)
                    + coefs[i][1] * coefs[j][1] * get(gram, i + half, j + half)
                )
        for k in range(len(weights)):
            node = k % count
            factor = coefs[node % half][node // half]
            weights[k] = factor if weights[k] is None else weights[k] * factor
        gram, count = merged, half
    return weights


def kernel(
    gate, up, grad, out,
    hown, hb, gb, leaf, pbuf, wbuf, ar, cst, obuf,
    own_sem, gx_s, gx_r, hz_s, hz_r, gz_s, gz_r, gy_s, gy_r, sib_s, sib_r, hx_s, hx_r, ar_s, ar_r, oz_s, oz_r,
):
    dp = lax.axis_index("dp")
    t = lax.axis_index("tensor")
    x, z = lax.div(dp, NZ), lax.rem(dp, NZ)
    y, core = lax.div(t, 2), lax.rem(t, 2)
    sib = y * 2 + 1 - core

    def xo(k):
        return lax.rem(x + k, NX)

    def zo(k):
        return lax.rem(z + k, NZ)

    def to(k):
        return lax.rem(t + k, NT)

    def yo(k):
        return lax.rem(y + k, 4) * 2 + core

    def at_x(k):
        return (xo(k) * NZ + z, t)

    def at_z(k):
        return (x * NZ + zo(k), t)

    def at_t(rank):
        return (dp, rank)

    def remote(src, dst, send, recv, where):
        return pltpu.make_async_remote_copy(
            src_ref=src, dst_ref=dst, send_sem=send, recv_sem=recv, device_id=where, device_id_type=MESH
        )

    sent = []

    def send(src, dst, ss, rs, where):
        copy = remote(src, dst, ss, rs, where)
        copy.start()
        sent.append(copy)

    def arrived(dst, ss, rs):
        remote(dst, dst, ss, rs, at_x(1)).wait_recv()

    def gpart(zc, rank, lo=0, n=NX):
        return gb.at[pl.ds(lo, n), zc, pl.ds(pl.multiple_of(rank * TR, TR), TR), :]

    barrier = pltpu.get_barrier_semaphore()
    partners = [at_x(k) for k in range(1, NX)] + [at_z(k) for k in range(1, NZ)] + [at_t(to(k)) for k in range(1, NT)]
    for where in partners:
        pl.semaphore_signal(barrier, inc=1, device_id=where, device_id_type=MESH)
    pl.semaphore_wait(barrier, len(partners))

    rows_t = pl.ds(pl.multiple_of(t * TR, TR), TR)
    for k in range(1, NX):
        cols = pl.ds(pl.multiple_of(xo(k) * NB, NB), NB)
        send(grad.at[rows_t, cols], gb.at[x, z, rows_t, :], gx_s.at[k], gx_r.at[k], at_x(k))
    own_g = pltpu.make_async_copy(
        grad.at[rows_t, pl.ds(pl.multiple_of(x * NB, NB), NB)], gb.at[x, z, rows_t, :], own_sem.at[0]
    )
    own_g.start()

    for j in range(HID // 128):
        cols = slice(128 * j, 128 * j + 128)
        v = gate[:, cols].astype(jnp.float32)
        u = up[:, cols].astype(jnp.float32)
        h = v / (1.0 + jnp.exp(-v)) * u
        hown[cols, :] = h.T.astype(jnp.bfloat16)

    def hown_at(zc):
        return hown.at[pl.ds(pl.multiple_of(zc * MB, 16), MB), :]

    own_h = pltpu.make_async_copy(hown_at(z), hb.at[x, z], own_sem.at[1])
    own_h.start()

    def start_hz(k):
        send(hown_at(zo(k)), hb.at[x, z], hz_s.at[k], hz_r.at[k], at_z(k))

    def g_z(i):
        o = ORDER[i]
        zc = zo(o)
        if o == 0:
            own_g.wait()
            for k in range(1, NX):
                arrived(gb.at[xo(NX - k), z, rows_t, :], gx_s.at[k], gx_r.at[k])
            send(gpart(zc, t), gpart(zc, t), gz_s.at[0, 1], gz_r.at[0, 1], at_z(1))
            send(gpart(zc, t), gpart(zc, t), gz_s.at[1, 1], gz_r.at[1, 1], at_z(7))
        elif o == 4:
            arrived(gpart(zc, t, 0, 2), gz_s.at[0, 4], gz_r.at[0, 4])
            arrived(gpart(zc, t, 2, 2), gz_s.at[1, 4], gz_r.at[1, 4])
        else:
            way, step = (0, 8 - o) if o > 4 else (1, o)
            arrived(gpart(zc, t), gz_s.at[way, step], gz_r.at[way, step])
            part = (0, 4) if step < 3 else (2 * way, 2)
            send(
                gpart(zc, t, *part), gpart(zc, t, *part),
                gz_s.at[way, step + 1], gz_r.at[way, step + 1], at_z(1 if way == 0 else 7),
            )
        send(gpart(zc, t), gpart(zc, t), gy_s.at[0, o], gy_r.at[0, o], at_t(yo(1)))
        send(gpart(zc, t), gpart(zc, t), gy_s.at[1, o], gy_r.at[1, o], at_t(yo(3)))
        send(gpart(zc, t), gpart(zc, t), sib_s.at[0, o], sib_r.at[0, o], at_t(sib))

    def g_y(i):
        o = ORDER[i]
        zc = zo(o)
        for way in range(2):
            rank = yo(3 if way == 0 else 1)
            arrived(gpart(zc, rank), gy_s.at[way, o], gy_r.at[way, o])
            half = gpart(zc, rank, 2 * way, 2)
            send(half, half, gy_s.at[2 + way, o], gy_r.at[2 + way, o], at_t(yo(1 if way == 0 else 3)))
            whole = gpart(zc, rank)
            send(whole, whole, sib_s.at[1 + way, o], sib_r.at[1 + way, o], at_t(sib))

    def g_far(i):
        o = ORDER[i]
        zc = zo(o)
        for way in range(2):
            half = gpart(zc, yo(2), 2 * way, 2)
            arrived(half, gy_s.at[2 + way, o], gy_r.at[2 + way, o])
            send(half, half, sib_s.at[3 + way, o], sib_r.at[3 + way, o], at_t(sib))

    def h_z(i):
        o = ORDER[i]
        zc = zo(o)
        if o == 0:
            own_h.wait()
        else:
            arrived(hb.at[x, zc], hz_s.at[8 - o], hz_r.at[8 - o])
        send(hb.at[x, zc], hb.at[x, zc], hx_s.at[0, o], hx_r.at[0, o], at_x(1))
        send(hb.at[x, zc], hb.at[x, zc], hx_s.at[1, o], hx_r.at[1, o], at_x(3))

    def h_x(i):
        o = ORDER[i]
        zc = zo(o)
        for way in range(2):
            xs = xo(3 if way == 0 else 1)
            arrived(hb.at[xs, zc], hx_s.at[way, o], hx_r.at[way, o])
            half = hb.at[xs, zc, pl.ds(way * (MB // 2), MB // 2), :]
            send(half, half, hx_s.at[2 + way, o], hx_r.at[2 + way, o], at_x(1 if way == 0 else 3))

    def finish(i):
        o = ORDER[i]
        zc = zo(o)
        for way in range(2):
            half = hb.at[xo(2), zc, pl.ds(way * (MB // 2), MB // 2), :]
            arrived(half, hx_s.at[2 + way, o], hx_r.at[2 + way, o])
        other = 1 - 2 * core
        arrived(gpart(zc, sib), sib_s.at[0, o], sib_r.at[0, o])
        arrived(gpart(zc, yo(3) + other), sib_s.at[1, o], sib_r.at[1, o])
        arrived(gpart(zc, yo(1) + other), sib_s.at[2, o], sib_r.at[2, o])
        arrived(gpart(zc, yo(2) + other, 0, 2), sib_s.at[3, o], sib_r.at[3, o])
        arrived(gpart(zc, yo(2) + other, 2, 2), sib_s.at[4, o], sib_r.at[4, o])

        def product(k, _):
            xx = lax.div(k, 4)
            cols = pl.ds(pl.multiple_of(lax.rem(k, 4) * 256, 256), 256)
            leaf[zc, xx, :, cols] = jnp.dot(hb[xx, zc], gb[xx, zc, :, cols], preferred_element_type=jnp.float32)
            return 0

        lax.fori_loop(0, 16, product, 0)

        def gram(k, sums):
            rows = pl.ds(pl.multiple_of(k * 8, 8), 8)
            for c in range(NB // 128):
                vals = [leaf[zc, xx, rows, 128 * c:128 * c + 128] for xx in range(4)]
                sums = tuple(s + vals[a] * vals[b] for s, (a, b) in zip(sums, PAIRS4))
            return sums

        sums = lax.fori_loop(0, MB // 8, gram, (jnp.zeros((8, 128), jnp.float32),) * len(PAIRS4))
        for k, s in enumerate(sums):
            pbuf[0, k * 8 + zc] = s

    def all_sum(which):
        rows = jnp.sum(pbuf[which], axis=1)
        value = jnp.broadcast_to(jnp.sum(rows.T, axis=0, keepdims=True), (8, 128))
        for phase, (count, me) in enumerate(((NT, t), (NX, x), (NZ, z))):
            slots = ar.at[which, phase]
            slots[me] = value
            for k in range(1, count):
                where = (at_t(to(k)), at_x(k), at_z(k))[phase]
                send(slots.at[me], slots.at[me], ar_s.at[which, phase, k], ar_r.at[which, phase, k], where)
            for k in range(1, count):
                arrived(
                    slots.at[lax.rem(me + count - k, count)], ar_s.at[which, phase, k], ar_r.at[which, phase, k]
                )
            value = jnp.sum(slots[0:count], axis=0)
        return jnp.broadcast_to(value[0:1], (128, 128)).T

    pbuf[...] = jnp.zeros_like(pbuf)
    stages = ((g_z, 0), (g_y, 1), (g_far, 2), (h_z, 0), (h_x, 1), (finish, 3))
    for k in range(1, 5):
        start_hz(k)
        if k < 4:
            start_hz(8 - k)
    for i in range(NZ + 3):
        for stage, lag in stages:
            if 0 <= i - lag < NZ:
                stage(i - lag)

    table = all_sum(0)
    weights = tree_weights({pair: table[8 * k:8 * k + 8] for k, pair in enumerate(PAIRS4)}, 4)
    for zz in range(NZ):
        for xx in range(NX):
            wbuf[zz * 4 + xx] = jnp.broadcast_to(weights[xx][zz:zz + 1], (8, 128))

    def merge(k, sums):
        rows = pl.ds(pl.multiple_of(k * 8, 8), 8)
        for c in range(NB // 128):
            cols = slice(128 * c, 128 * c + 128)
            nodes = []
            for zz in range(NZ):
                parts = [wbuf[zz * 4 + xx] * leaf[zz, xx, rows, cols] for xx in range(NX)]
                node = (parts[0] + parts[1]) + (parts[2] + parts[3])
                leaf[zz, 0, rows, cols] = node
                nodes.append(node)
            sums = tuple(s + nodes[a] * nodes[b] for s, (a, b) in zip(sums, PAIRS8))
        return sums

    sums = lax.fori_loop(0, MB // 8, merge, (jnp.zeros((8, 128), jnp.float32),) * len(PAIRS8))
    for k, s in enumerate(sums):
        pbuf[1, k] = s

    table = all_sum(1)
    weights = tree_weights({pair: table[k:k + 1] for k, pair in enumerate(PAIRS8)}, 8)
    for k in (4, 3, 5, 2, 6, 1, 7, 0):
        zt = zo(k)
        cols = pl.ds(pl.multiple_of(zt * 128, 128), 128)
        total = weights[0] * leaf[0, 0, :, cols]
        for zz in range(1, NZ):
            total = total + weights[zz] * leaf[zz, 0, :, cols]
        cst[k] = total.astype(jnp.bfloat16)
        if k:
            send(cst.at[k], obuf.at[z], oz_s.at[k], oz_r.at[k], at_z(k))
    out[pl.ds(pl.multiple_of(z * MB, 16), MB), :] = cst[0]
    for k in range(1, NZ):
        zs = zo(NZ - k)
        arrived(obuf.at[zs], oz_s.at[k], oz_r.at[k])
        out[pl.ds(pl.multiple_of(zs * MB, 16), MB), :] = obuf[zs]
    for copy in sent:
        copy.wait_send()


def body(gate_input, up_input, grad_out):
    dma = pltpu.SemaphoreType.DMA
    vmem = pl.BlockSpec(memory_space=pltpu.VMEM)
    return pl.pallas_call(
        kernel,
        out_shape=jax.ShapeDtypeStruct((HID, 128), jnp.bfloat16),
        in_specs=[vmem, vmem, pl.BlockSpec(memory_space=pl.ANY)],
        out_specs=vmem,
        scratch_shapes=[
            pltpu.VMEM((HID, TOK), jnp.bfloat16),
            pltpu.VMEM((NX, NZ, MB, TOK), jnp.bfloat16),
            pltpu.VMEM((NX, NZ, TOK, NB), jnp.bfloat16),
            pltpu.VMEM((NZ, NX, MB, NB), jnp.float32),
            pltpu.VMEM((2, 128, 8, 128), jnp.float32),
            pltpu.VMEM((NZ * NX, 8, 128), jnp.float32),
            pltpu.VMEM((2, 3, 8, 8, 128), jnp.float32),
            pltpu.VMEM((NZ, MB, 128), jnp.bfloat16),
            pltpu.VMEM((NZ, MB, 128), jnp.bfloat16),
            dma((2,)),
            dma((NX,)), dma((NX,)),
            dma((NZ,)), dma((NZ,)),
            dma((2, 5)), dma((2, 5)),
            dma((4, NZ)), dma((4, NZ)),
            dma((5, NZ)), dma((5, NZ)),
            dma((4, NZ)), dma((4, NZ)),
            dma((2, 3, 8)), dma((2, 3, 8)),
            dma((NZ,)), dma((NZ,)),
        ],
        compiler_params=pltpu.CompilerParams(
            collective_id=0, has_side_effects=True, vmem_limit_bytes=62 * 1024 * 1024
        ),
        cost_estimate=pl.CostEstimate(flops=3_760_000_000, bytes_accessed=5_000_000, transcendentals=460_000),
    )(gate_input, up_input, grad_out)


def solution(mesh):
    placed = (P("dp", "tensor"), P("dp", "tensor"), P("dp", None))
    return jax.shard_map(
        body, mesh=mesh, in_specs=placed, out_specs=P("tensor", "dp"), check_vma=False
    )
```

time: 627 us -> 158 us (0.25)
  waiting for transfers between devices: 361 us -> 0 us
  Pallas kernels: 0 us -> 156 us
  blocking collectives: 110 us -> 0 us
  starting transfers between devices: 51.7 us -> 0 us
  other arithmetic: 45 us -> 0 us
  between operations: 25 us -> 0.01 us
  matrix products: 18.4 us -> 0 us
  local copies, waits for them, and re-layouts: 15.5 us -> 1.82 us
    ppermute x20 -> x0, waiting for transfers between devices: 361 us -> none  [partner(): return lax.ppermute(block, axis, route)]
    pallas_call x0 -> x1, Pallas kernels: none -> 156 us  [body(): pl.pallas_call(kernel, out_shape=jax.ShapeDtypeStruct((HID, 128), jnp.bfl...]
    psum x5 -> x0, blocking collectives: 110 us -> none  [group_totals(): return lax.psum(partials, 'tensor')]
    ppermute x20 -> x0, starting transfers between devices: 51.7 us -> none  [partner(): return lax.ppermute(block, axis, route)]
    convert_element_type x5 -> x0, other arithmetic: 23.2 us -> none  [combine_section(): return merged.astype(jnp.bfloat16)]
    dot_general x2 -> x0, matrix products: 18.4 us -> none  [outer_grad(): lax.dot_general(hidden, grad_cols, (((0,), (0,)), ((), ())), preferred_el...]
    reduce_sum x4 -> x0, other arithmetic: 12 us -> none  [combine_section(): self_kept = jnp.sum(kept_f * kept_f)]
    dynamic_slice x4 -> x0, local copies, waits for them, and re-layouts: 7.61 us -> none  [body(): lax.dynamic_slice_in_dim(current, (1 - upper_half) * half_cols, half_cols...]
  transfers between devices with their start and end apart: 20 -> 0, of which waited for: 20 -> 0; matrix products, arithmetic and copies ran while one was open for 0% -> 0% of each run, Pallas kernels for 0% -> 0%
where the time goes in v1:
time: 158 us
  Pallas kernels  156 us (99%)
  local copies, waits for them, and re-layouts  1.82 us (1%)
    pallas_call x1, Pallas kernels, body(): pl.pallas_call(kernel, out_shape=jax.ShapeDtypeStruct((HID, 128), jnp.bfl...  156 us

profile of v1, /device:TPU:1, one launch (start us, length us, event | category | flops | bytes accessed | tf_op | source)
XLA Modules:
  0.0 157.7 jit_solution(13471490218367505113)
XLA Ops:
  0.0 155.8 %shard_map.37 = bf16[1792,128]{1,0:T(8,128)(2,1)} custom-call(bf16[256,1792]{1,0:T(8,128)(2,1)} %gate.1, bf16[256,1792]{1,0:T(8,128)(2,1)} %up.1, bf16[256,4096]{1,0:T(8,128)(2,1)} %grad.1), custom_call_target="tpu_custom_call" | custom-call | flops 3760000000 | bytes 5000000 | tf_op jit(solution)/shard_map/pallas_call | solution.py:305
  155.8 1.8 %copy.5 = bf16[1792,128]{1,0:T(8,128)(2,1)} copy(bf16[1792,128]{1,0:T(8,128)(2,1)} %shard_map.37) | data formatting | bytes 917504

commit v2 on v1

v2 whole, which is shorter than its diff:
```python
import functools

import jax
import jax.numpy as jnp
from jax import lax
from jax.experimental import pallas as pl
from jax.experimental.pallas import tpu as pltpu
from jax.sharding import PartitionSpec as P

epsilon = 1e-06
MESH = pl.DeviceIdType.MESH
NX, NZ, NT = 4, 8, 8
TOK = 256
HID = 1792
MB = HID // NZ
NB = 1024
TR = TOK // NT
HR = TOK // 2
CS = 768
ORDER = (0, 7, 1, 6, 2, 5, 3, 4)
SCHEDULE = (
    "h0", "s1", "s7", "s2", "s6", "q0", "r0", "h1", "h2", "x0", "y0", "h3", "h4", "x1", "x2", "f0",
    "q1", "q2", "x3", "x4", "c0", "y1", "r1", "r2", "y2", "f1",
    "q3", "q4", "s3", "s5", "f2", "c1", "y3", "r3", "r4", "c2", "y4", "f3",
    "q5", "q6", "s4", "f4", "h5", "h6", "c3", "x5", "y5", "r5", "r6", "x6", "y6", "c4",
    "q7", "f5", "r7", "f6", "h7", "c5", "y7", "x7", "c6", "f7", "c7",
)
PAIRS4 = [(i, j) for i in range(4) for j in range(i, 4)]
ALL4 = [(i, j) for i in range(4) for j in range(4)]
PAIRS8 = [(i, j) for i in range(8) for j in range(i, 8)]


def pair_coefs(aa, bb, ab):
    aa = jnp.maximum(aa, 0.0)
    bb = jnp.maximum(bb, 0.0)
    bound = jnp.sqrt(aa) * jnp.sqrt(bb)
    ab = jnp.clip(ab, -bound, bound)
    return 1.0 - ab / (2.0 * (aa + epsilon)), 1.0 - ab / (2.0 * (bb + epsilon))


def tree_weights(gram, count):
    def get(table, i, j):
        return table[(min(i, j), max(i, j))]

    weights = [None] * count
    while count > 1:
        half = count // 2
        coefs = [
            pair_coefs(gram[(j, j)], gram[(j + half, j + half)], get(gram, j, j + half))
            for j in range(half)
        ]
        merged = {}
        for i in range(half):
            for j in range(i, half):
                merged[(i, j)] = (
                    coefs[i][0] * coefs[j][0] * get(gram, i, j)
                    + coefs[i][0] * coefs[j][1] * get(gram, i, j + half)
                    + coefs[i][1] * coefs[j][0] * get(gram, i + half, j)
                    + coefs[i][1] * coefs[j][1] * get(gram, i + half, j + half)
                )
        for k in range(len(weights)):
            node = k % count
            factor = coefs[node % half][node // half]
            weights[k] = factor if weights[k] is None else weights[k] * factor
        gram, count = merged, half
    return weights


def kernel(
    gate, up, grad, out,
    hown, hb, gb, leaf, pbuf, wbuf, ar, cst, obuf,
    own_sem, gx_s, gx_r, hz_s, hz_r, gz_s, gz_r, gy_s, gy_r, sib_s, sib_r, hx_s, hx_r, ar_s, ar_r, oz_s, oz_r,
):
    dp = lax.axis_index("dp")
    t = lax.axis_index("tensor")
    x, z = lax.div(dp, NZ), lax.rem(dp, NZ)
    y, core = lax.div(t, 2), lax.rem(t, 2)
    sib = y * 2 + 1 - core

    def xo(k):
        return lax.rem(x + k, NX)

    def zo(k):
        return lax.rem(z + k, NZ)

    def to(k):
        return lax.rem(t + k, NT)

    def yo(k):
        return lax.rem(y + k, 4) * 2 + core

    def at_x(k):
        return (xo(k) * NZ + z, t)

    def at_z(k):
        return (x * NZ + zo(k), t)

    def at_t(rank):
        return (dp, rank)

    def remote(src, dst, send, recv, where):
        return pltpu.make_async_remote_copy(
            src_ref=src, dst_ref=dst, send_sem=send, recv_sem=recv, device_id=where, device_id_type=MESH
        )

    sent, done = [], []

    def send(src, dst, ss, rs, where):
        copy = remote(src, dst, ss, rs, where)
        copy.start()
        sent.append(copy)

    def arrived(dst, ss, rs):
        remote(dst, dst, ss, rs, at_x(1)).wait_recv()

    def quarter(zc, yy, lo=0, n=NX, c=core):
        rows = pl.ds(pl.multiple_of(c * HR + lax.rem(y + yy, 4) * TR, TR), TR)
        return gb.at[pl.ds(lo, n), zc, rows, pl.ds(0, CS)]

    def rest(zc, lo=0, n=NX, c=core):
        return gb.at[pl.ds(lo, n), zc, pl.ds(pl.multiple_of(c * HR, HR), HR), pl.ds(CS, NB - CS)]

    barrier = pltpu.get_barrier_semaphore()
    partners = [at_x(k) for k in range(1, NX)] + [at_z(k) for k in range(1, NZ)] + [at_t(to(k)) for k in range(1, NT)]
    for where in partners:
        pl.semaphore_signal(barrier, inc=1, device_id=where, device_id_type=MESH)

    for j in range(HID // 128):
        cols = slice(128 * j, 128 * j + 128)
        v = gate[:, cols].astype(jnp.float32)
        u = up[:, cols].astype(jnp.float32)
        h = v / (1.0 + jnp.exp(-v)) * u
        hown[cols, :] = h.T.astype(jnp.bfloat16)

    pbuf[...] = jnp.zeros_like(pbuf)
    pl.semaphore_wait(barrier, len(partners))

    def grad_at(p, xs):
        if p == 0:
            rows, lo, n = pl.ds(pl.multiple_of(core * HR + y * TR, TR), TR), 0, CS
        else:
            rows, lo, n = pl.ds(pl.multiple_of(core * HR, HR), HR), CS, NB - CS
        return grad.at[rows, pl.ds(pl.multiple_of(xs * NB + lo, 128), n)]

    def part_at(p, zc, lo=0, n=NX):
        return quarter(zc, 0, lo, n) if p == 0 else rest(zc, lo, n)

    own_g = []
    for p in range(2):
        for k in (1, 3, 2):
            dst = part_at(p, z, x, 1)
            send(grad_at(p, xo(k)), dst.at[0], gx_s.at[p, k], gx_r.at[p, k], at_x(k))
        own_g.append(pltpu.make_async_copy(grad_at(p, x), part_at(p, z, x, 1).at[0], own_sem.at[p]))
        own_g[p].start()

    def hown_at(zc):
        return hown.at[pl.ds(pl.multiple_of(zc * MB, 16), MB), :]

    own_h = pltpu.make_async_copy(hown_at(z), hb.at[x, z], own_sem.at[2])
    own_h.start()

    def start_hz(k):
        send(hown_at(zo(k)), hb.at[x, z], hz_s.at[k], hz_r.at[k], at_z(k))

    def to_sib(part, slot, o):
        send(part, part, sib_s.at[slot, o], sib_r.at[slot, o], at_t(sib))

    def g_z(p, i):
        o = ORDER[i]
        zc = zo(o)

        def come(way, step, lo, n):
            arrived(part_at(p, zc, lo, n), gz_s.at[way, step, p], gz_r.at[way, step, p])

        def go(way, step, lo, n):
            part = part_at(p, zc, lo, n)
            send(part, part, gz_s.at[way, step, p], gz_r.at[way, step, p], at_z(1 if way == 0 else 7))

        if o == 0:
            own_g[p].wait()
            for k in range(1, NX):
                arrived(part_at(p, z, xo(NX - k), 1).at[0], gx_s.at[p, k], gx_r.at[p, k])
            go(0, 1, 0, NX)
            go(1, 1, 0, NX)
        elif o == 4:
            come(0, 4, 0, 2)
            come(1, 4, 2, 2)
        else:
            way, step = (0, 8 - o) if o > 4 else (1, o)
            come(way, step, 0, NX)
            if step < 3:
                go(way, step + 1, 0, NX)
            else:
                go(way, 4, 2 * way, 2)
        if p == 0:
            part = quarter(zc, 0)
            send(part, part, gy_s.at[0, o], gy_r.at[0, o], at_t(yo(1)))
            send(part, part, gy_s.at[1, o], gy_r.at[1, o], at_t(yo(3)))
        to_sib(part_at(p, zc), p, o)

    def g_y(i):
        o = ORDER[i]
        zc = zo(o)
        for way in range(2):
            source = 3 if way == 0 else 1
            arrived(quarter(zc, source), gy_s.at[way, o], gy_r.at[way, o])
            part = quarter(zc, source, 2 * way, 2)
            send(part, part, gy_s.at[2 + way, o], gy_r.at[2 + way, o], at_t(yo(4 - source)))
            to_sib(quarter(zc, source), 2 + way, o)

    def g_far(i):
        o = ORDER[i]
        zc = zo(o)
        for way in range(2):
            part = quarter(zc, 2, 2 * way, 2)
            arrived(part, gy_s.at[2 + way, o], gy_r.at[2 + way, o])
            to_sib(part, 4 + way, o)

    def h_z(i):
        o = ORDER[i]
        zc = zo(o)
        if o == 0:
            own_h.wait()
        else:
            arrived(hb.at[x, zc], hz_s.at[8 - o], hz_r.at[8 - o])
        send(hb.at[x, zc], hb.at[x, zc], hx_s.at[0, o], hx_r.at[0, o], at_x(1))
        send(hb.at[x, zc], hb.at[x, zc], hx_s.at[1, o], hx_r.at[1, o], at_x(3))

    def h_x(i):
        o = ORDER[i]
        zc = zo(o)
        for way in range(2):
            xs = xo(3 if way == 0 else 1)
            arrived(hb.at[xs, zc], hx_s.at[way, o], hx_r.at[way, o])
            half = hb.at[xs, zc, pl.ds(way * (MB // 2), MB // 2), :]
            send(half, half, hx_s.at[2 + way, o], hx_r.at[2 + way, o], at_x(1 if way == 0 else 3))

    def finish(i):
        o = ORDER[i]
        zc = zo(o)
        for way in range(2):
            half = hb.at[xo(2), zc, pl.ds(way * (MB // 2), MB // 2), :]
            arrived(half, hx_s.at[2 + way, o], hx_r.at[2 + way, o])
        c = 1 - core
        parts = [quarter(zc, 0, c=c), rest(zc, c=c), quarter(zc, 3, c=c), quarter(zc, 1, c=c)]
        parts += [quarter(zc, 2, 0, 2, c=c), quarter(zc, 2, 2, 2, c=c)]
        for slot, part in enumerate(parts):
            arrived(part, sib_s.at[slot, o], sib_r.at[slot, o])

        def product(k, _):
            xx = lax.div(k, 4)
            cols = pl.ds(pl.multiple_of(lax.rem(k, 4) * 256, 256), 256)
            leaf[zc, xx, :, cols] = jnp.dot(hb[xx, zc], gb[xx, zc, :, cols], preferred_element_type=jnp.float32)
            return 0

        lax.fori_loop(0, 16, product, 0)

        def products(za, zb, pairs):
            def gram(k, sums):
                rows = pl.ds(pl.multiple_of(k * 8, 8), 8)
                for c in range(NB // 128):
                    cols = slice(128 * c, 128 * c + 128)
                    a = [leaf[za, xx, rows, cols] for xx in range(NX)]
                    b = a if za is zb else [leaf[zb, xx, rows, cols] for xx in range(NX)]
                    sums = tuple(s + a[m] * b[n] for s, (m, n) in zip(sums, pairs))
                return sums

            return lax.fori_loop(0, MB // 8, gram, (jnp.zeros((8, 128), jnp.float32),) * len(pairs))

        def keep(m, n, low, gap, value):
            pbuf[pl.ds((m * 4 + n) * 64 + gap * 8 + low, 1), :] = jnp.sum(value, axis=0, keepdims=True)

        for (m, n), value in zip(PAIRS4, products(zc, zc, PAIRS4)):
            keep(m, n, zc, 0, value)
            if m != n:
                keep(n, m, zc, 0, value)
        for other in done:
            zd = zo(other)
            low, first = jnp.minimum(zc, zd), jnp.where(zc < zd, 1, 0)
            gap = zc + zd - 2 * low
            for (m, n), value in zip(ALL4, products(zc, zd, ALL4)):
                keep(first * m + (1 - first) * n, first * n + (1 - first) * m, low, gap, value)
        done.append(o)

    def all_sum(value):
        for phase, (count, me) in enumerate(((NT, t), (NX, x), (NZ, z))):
            slots = ar.at[phase]
            slots[me] = value
            for k in range(1, count):
                where = (at_t(to(k)), at_x(k), at_z(k))[phase]
                send(slots.at[me], slots.at[me], ar_s.at[phase, k], ar_r.at[phase, k], where)
            for k in range(1, count):
                arrived(slots.at[lax.rem(me + count - k, count)], ar_s.at[phase, k], ar_r.at[phase, k])
            value = jnp.sum(slots[0:count], axis=0)
        return value

    stages = {
        "s": start_hz, "q": functools.partial(g_z, 0), "r": functools.partial(g_z, 1), "y": g_y, "f": g_far,
        "h": h_z, "x": h_x, "c": finish,
    }
    for step in SCHEDULE:
        stages[step[0]](int(step[1]))

    tile = all_sum(
        jnp.concatenate(
            [jnp.sum(pbuf[128 * k:128 * k + 128, :].T, axis=0, keepdims=True) for k in range(8)], axis=0
        )
    )
    spread = [jnp.broadcast_to(tile[k:k + 1], (128, 128)).T for k in range(8)]
    table = [spread[k // 2][64 * (k % 2):64 * (k % 2) + 64] for k in range(16)]
    lower = tree_weights({(m, n): table[m * 4 + n][0:8] for m, n in PAIRS4}, 4)
    nodes = []
    for gap in range(NZ):
        shifted = [w if gap == 0 else jnp.concatenate([w[gap:], w[:gap]], axis=0) for w in lower]
        rows = slice(8 * gap, 8 * gap + 8)
        total = None
        for m in range(4):
            inner = sum(shifted[n] * table[m * 4 + n][rows] for n in range(4))
            total = lower[m] * inner if total is None else total + lower[m] * inner
        nodes.append(total)
    upper = tree_weights({(i, j): nodes[j - i][i:i + 1] for i, j in PAIRS8}, 8)
    for zz in range(NZ):
        for xx in range(NX):
            wbuf[zz * 4 + xx] = jnp.broadcast_to(lower[xx][zz:zz + 1] * upper[zz], (8, 128))

    for k in (4, 3, 5, 2, 6, 1, 7, 0):
        cols = pl.ds(pl.multiple_of(zo(k) * 128, 128), 128)

        def combine(g, _, k=k, cols=cols):
            totals = [jnp.zeros((8, 128), jnp.float32)] * 4
            for r in range(NZ * NX):
                w = wbuf[r]
                for q in range(4):
                    rows = pl.ds(pl.multiple_of(g * 32 + 8 * q, 8), 8)
                    totals[q] = totals[q] + w * leaf[r // 4, r % 4, rows, cols]
            block = jnp.concatenate(totals, axis=0).astype(jnp.bfloat16)
            cst[k, pl.ds(pl.multiple_of(g * 32, 32), 32), :] = block
            return 0

        lax.fori_loop(0, MB // 32, combine, 0)
        if k:
            send(cst.at[k], obuf.at[z], oz_s.at[k], oz_r.at[k], at_z(k))
    out[pl.ds(pl.multiple_of(z * MB, 16), MB), :] = cst[0]
    for k in range(1, NZ):
        zs = zo(NZ - k)
        arrived(obuf.at[zs], oz_s.at[k], oz_r.at[k])
        out[pl.ds(pl.multiple_of(zs * MB, 16), MB), :] = obuf[zs]
    for copy in sent:
        copy.wait_send()


def body(gate_input, up_input, grad_out):
    dma = pltpu.SemaphoreType.DMA
    vmem = pl.BlockSpec(memory_space=pltpu.VMEM)
    return pl.pallas_call(
        kernel,
        out_shape=jax.ShapeDtypeStruct((HID, 128), jnp.bfloat16),
        in_specs=[vmem, vmem, pl.BlockSpec(memory_space=pl.ANY)],
        out_specs=vmem,
        scratch_shapes=[
            pltpu.VMEM((HID, TOK), jnp.bfloat16),
            pltpu.VMEM((NX, NZ, MB, TOK), jnp.bfloat16),
            pltpu.VMEM((NX, NZ, TOK, NB), jnp.bfloat16),
            pltpu.VMEM((NZ, NX, MB, NB), jnp.float32),
            pltpu.VMEM((1024, 128), jnp.float32),
            pltpu.VMEM((NZ * NX, 8, 128), jnp.float32),
            pltpu.VMEM((3, 8, 8, 128), jnp.float32),
            pltpu.VMEM((NZ, MB, 128), jnp.bfloat16),
            pltpu.VMEM((NZ, MB, 128), jnp.bfloat16),
            dma((3,)),
            dma((2, NX)), dma((2, NX)),
            dma((NZ,)), dma((NZ,)),
            dma((2, 5, 2)), dma((2, 5, 2)),
            dma((4, NZ)), dma((4, NZ)),
            dma((6, NZ)), dma((6, NZ)),
            dma((4, NZ)), dma((4, NZ)),
            dma((3, 8)), dma((3, 8)),
            dma((NZ,)), dma((NZ,)),
        ],
        compiler_params=pltpu.CompilerParams(
            collective_id=0, has_side_effects=True, vmem_limit_bytes=62 * 1024 * 1024
        ),
        cost_estimate=pl.CostEstimate(flops=3_760_000_000, bytes_accessed=5_000_000, transcendentals=460_000),
    )(gate_input, up_input, grad_out)


def solution(mesh):
    placed = (P("dp", "tensor"), P("dp", "tensor"), P("dp", None))
    return jax.shard_map(
        body, mesh=mesh, in_specs=placed, out_specs=P("tensor", "dp"), check_vma=False
    )
```

time: 158 us -> 144 us (0.911)
  Pallas kernels: 156 us -> 142 us
    pallas_call x1, Pallas kernels: 156 us -> 142 us  [body(): pl.pallas_call(kernel, out_shape=jax.ShapeDtypeStruct((HID, 128), jnp.bfl...]
where the time goes in v2:
time: 144 us
  Pallas kernels  142 us (99%)
  local copies, waits for them, and re-layouts  1.82 us (1%)
    pallas_call x1, Pallas kernels, body(): pl.pallas_call(kernel, out_shape=jax.ShapeDtypeStruct((HID, 128), jnp.bfl...  142 us

profile of v2, /device:TPU:1, one launch (start us, length us, event | category | flops | bytes accessed | tf_op | source)
XLA Modules:
  0.0 144.1 jit_solution(12654343148434638858)
XLA Ops:
  0.0 142.3 %shard_map.37 = bf16[1792,128]{1,0:T(8,128)(2,1)} custom-call(bf16[256,1792]{1,0:T(8,128)(2,1)} %gate.1, bf16[256,1792]{1,0:T(8,128)(2,1)} %up.1, bf16[256,4096]{1,0:T(8,128)(2,1)} %grad.1), custom_call_target="tpu_custom_call" | custom-call | flops 3760000000 | bytes 5000000 | tf_op jit(solution)/shard_map/pallas_call | solution.py:355
  142.3 1.8 %copy.5 = bf16[1792,128]{1,0:T(8,128)(2,1)} copy(bf16[1792,128]{1,0:T(8,128)(2,1)} %shard_map.37) | data formatting | bytes 917504

commit v3 on v2

--- a/solution.py
+++ b/solution.py
@@ -16,6 +16,8 @@
 NB = 1024
 TR = TOK // NT
 HR = TOK // 2
+DB = 1024
+GB = 4
 CS = 768
 ORDER = (0, 7, 1, 6, 2, 5, 3, 4)
 SCHEDULE = (
@@ -25,50 +27,49 @@
     "q5", "q6", "s4", "f4", "h5", "h6", "c3", "x5", "y5", "r5", "r6", "x6", "y6", "c4",
     "q7", "f5", "r7", "f6", "h7", "c5", "y7", "x7", "c6", "f7", "c7",
 )
-PAIRS4 = [(i, j) for i in range(4) for j in range(i, 4)]
-ALL4 = [(i, j) for i in range(4) for j in range(4)]
-PAIRS8 = [(i, j) for i in range(8) for j in range(i, 8)]
-
-
-def pair_coefs(aa, bb, ab):
-    aa = jnp.maximum(aa, 0.0)
-    bb = jnp.maximum(bb, 0.0)
+TREE_BITS = (2, 1, 16, 8, 4)
+
+
+def pair_coef(aa, bb, ab):
+    aa, bb = jnp.maximum(aa, 0.0), jnp.maximum(bb, 0.0)
     bound = jnp.sqrt(aa) * jnp.sqrt(bb)
-    ab = jnp.clip(ab, -bound, bound)
-    return 1.0 - ab / (2.0 * (aa + epsilon)), 1.0 - ab / (2.0 * (bb + epsilon))
-
-
-def tree_weights(gram, count):
-    def get(table, i, j):
-        return table[(min(i, j), max(i, j))]
-
-    weights = [None] * count
-    while count > 1:
-        half = count // 2
-        coefs = [
-            pair_coefs(gram[(j, j)], gram[(j + half, j + half)], get(gram, j, j + half))
-            for j in range(half)
-        ]
-        merged = {}
-        for i in range(half):
-            for j in range(i, half):
-                merged[(i, j)] = (
-                    coefs[i][0] * coefs[j][0] * get(gram, i, j)
-                    + coefs[i][0] * coefs[j][1] * get(gram, i, j + half)
-                    + coefs[i][1] * coefs[j][0] * get(gram, i + half, j)
-                    + coefs[i][1] * coefs[j][1] * get(gram, i + half, j + half)
-                )
-        for k in range(len(weights)):
-            node = k % count
-            factor = coefs[node % half][node // half]
-            weights[k] = factor if weights[k] is None else weights[k] * factor
-        gram, count = merged, half
+    return 1.0 - jnp.clip(ab, -bound, bound) / (2.0 * (aa + epsilon))
+
+
+def swap(value, index, bit, axis):
+    size = value.shape[axis]
+    return jnp.where(
+        (index & bit) != 0, pltpu.roll(value, bit, axis), pltpu.roll(value, size - bit, axis)
+    )
+
+
+def leaf_weights(gram):
+    row = lax.broadcasted_iota(jnp.int32, gram.shape, 0)
+    lane = lax.broadcasted_iota(jnp.int32, gram.shape, 1)
+    weights = jnp.ones(gram.shape, jnp.float32)
+    for bit in TREE_BITS:
+        own = jnp.where(row == lane, gram, 0.0)
+        pair = jnp.where((row ^ bit) == lane, gram, 0.0)
+        far = swap(own, row, bit, 0)
+        far_t = swap(own, lane, bit, 1)
+        down = pair_coef(
+            jnp.sum(own, axis=1, keepdims=True), jnp.sum(far, axis=1, keepdims=True),
+            jnp.sum(pair, axis=1, keepdims=True),
+        )
+        across = pair_coef(
+            jnp.sum(own, axis=0, keepdims=True), jnp.sum(far_t, axis=0, keepdims=True),
+            jnp.sum(pair, axis=0, keepdims=True),
+        )
+        weights = weights * down
+        gram = gram * down * across
+        gram = gram + swap(gram, row, bit, 0)
+        gram = gram + swap(gram, lane, bit, 1)
     return weights
 
 
 def kernel(
     gate, up, grad, out,
-    hown, hb, gb, leaf, pbuf, wbuf, ar, cst, obuf,
+    hown, hb, gb, leaf, acc, wbuf, ar, cst, obuf,
     own_sem, gx_s, gx_r, hz_s, hz_r, gz_s, gz_r, gy_s, gy_r, sib_s, sib_r, hx_s, hx_r, ar_s, ar_r, oz_s, oz_r,
 ):
     dp = lax.axis_index("dp")
@@ -103,7 +104,7 @@
             src_ref=src, dst_ref=dst, send_sem=send, recv_sem=recv, device_id=where, device_id_type=MESH
         )
 
-    sent, done = [], []
+    sent = []
 
     def send(src, dst, ss, rs, where):
         copy = remote(src, dst, ss, rs, where)
@@ -132,7 +133,6 @@
         h = v / (1.0 + jnp.exp(-v)) * u
         hown[cols, :] = h.T.astype(jnp.bfloat16)
 
-    pbuf[...] = jnp.zeros_like(pbuf)
     pl.semaphore_wait(barrier, len(partners))
 
     def grad_at(p, xs):
@@ -248,39 +248,18 @@
             arrived(part, sib_s.at[slot, o], sib_r.at[slot, o])
 
         def product(k, _):
-            xx = lax.div(k, 4)
-            cols = pl.ds(pl.multiple_of(lax.rem(k, 4) * 256, 256), 256)
-            leaf[zc, xx, :, cols] = jnp.dot(hb[xx, zc], gb[xx, zc, :, cols], preferred_element_type=jnp.float32)
+            xx = 2 * lax.div(k, NB // DB)
+            cols = pl.ds(pl.multiple_of(lax.rem(k, NB // DB) * DB, DB), DB)
+            first, second = (
+                jnp.dot(hb[xx + m, zc], gb[xx + m, zc, :, cols], preferred_element_type=jnp.float32) for m in range(2)
+            )
+            rows = pl.ds(pl.multiple_of(zc * 32 + xx * 8, 16), 16)
+            for g in range(MB // 8):
+                both = jnp.concatenate([first[8 * g:8 * g + 8], second[8 * g:8 * g + 8]], axis=0)
+                leaf[g, rows, cols] = both.astype(jnp.bfloat16)
             return 0
 
-        lax.fori_loop(0, 16, product, 0)
-
-        def products(za, zb, pairs):
-            def gram(k, sums):
-                rows = pl.ds(pl.multiple_of(k * 8, 8), 8)
-                for c in range(NB // 128):
-                    cols = slice(128 * c, 128 * c + 128)
-                    a = [leaf[za, xx, rows, cols] for xx in range(NX)]
-                    b = a if za is zb else [leaf[zb, xx, rows, cols] for xx in range(NX)]
-                    sums = tuple(s + a[m] * b[n] for s, (m, n) in zip(sums, pairs))
-                return sums
-
-            return lax.fori_loop(0, MB // 8, gram, (jnp.zeros((8, 128), jnp.float32),) * len(pairs))
-
-        def keep(m, n, low, gap, value):
-            pbuf[pl.ds((m * 4 + n) * 64 + gap * 8 + low, 1), :] = jnp.sum(value, axis=0, keepdims=True)
-
-        for (m, n), value in zip(PAIRS4, products(zc, zc, PAIRS4)):
-            keep(m, n, zc, 0, value)
-            if m != n:
-                keep(n, m, zc, 0, value)
-        for other in done:
-            zd = zo(other)
-            low, first = jnp.minimum(zc, zd), jnp.where(zc < zd, 1, 0)
-            gap = zc + zd - 2 * low
-            for (m, n), value in zip(ALL4, products(zc, zd, ALL4)):
-                keep(first * m + (1 - first) * n, first * n + (1 - first) * m, low, gap, value)
-        done.append(o)
+        lax.fori_loop(0, 2 * NB // DB, product, 0)
 
     def all_sum(value):
         for phase, (count, me) in enumerate(((NT, t), (NX, x), (NZ, z))):
@@ -301,38 +280,43 @@
     for step in SCHEDULE:
         stages[step[0]](int(step[1]))
 
-    tile = all_sum(
-        jnp.concatenate(
-            [jnp.sum(pbuf[128 * k:128 * k + 128, :].T, axis=0, keepdims=True) for k in range(8)], axis=0
-        )
-    )
-    spread = [jnp.broadcast_to(tile[k:k + 1], (128, 128)).T for k in range(8)]
-    table = [spread[k // 2][64 * (k % 2):64 * (k % 2) + 64] for k in range(16)]
-    lower = tree_weights({(m, n): table[m * 4 + n][0:8] for m, n in PAIRS4}, 4)
-    nodes = []
-    for gap in range(NZ):
-        shifted = [w if gap == 0 else jnp.concatenate([w[gap:], w[:gap]], axis=0) for w in lower]
-        rows = slice(8 * gap, 8 * gap + 8)
+    acc[...] = jnp.zeros_like(acc)
+
+    def gram(k, _):
         total = None
-        for m in range(4):
-            inner = sum(shifted[n] * table[m * 4 + n][rows] for n in range(4))
-            total = lower[m] * inner if total is None else total + lower[m] * inner
-        nodes.append(total)
-    upper = tree_weights({(i, j): nodes[j - i][i:i + 1] for i, j in PAIRS8}, 8)
-    for zz in range(NZ):
-        for xx in range(NX):
-            wbuf[zz * 4 + xx] = jnp.broadcast_to(lower[xx][zz:zz + 1] * upper[zz], (8, 128))
+        for g in range(GB):
+            rows = leaf[k * GB + g]
+            part = lax.dot_general(rows, rows, (((1,), (1,)), ((), ())), preferred_element_type=jnp.float32)
+            total = part if total is None else total + part
+        acc[...] += total
+        return 0
+
+    lax.fori_loop(0, MB // 8 // GB, gram, 0)
+    index = [lax.broadcasted_iota(jnp.int32, (256, 256), axis) for axis in range(2)]
+    like = jnp.where(lax.rem(index[0], 8) == lax.rem(index[1], 8), acc[...], 0.0)
+    like = jnp.sum(like.reshape(32, 8, 256), axis=1)
+    index = [lax.broadcasted_iota(jnp.int32, (256, 128), axis) for axis in range(2)]
+    pick = jnp.where(lax.div(index[0], 8) == index[1], 1.0, 0.0).astype(jnp.float32)
+    local = jnp.dot(like, pick, precision=lax.Precision.HIGHEST, preferred_element_type=jnp.float32)
+    tile = local[0:8]
+    for q in range(1, 4):
+        tile = tile + pltpu.roll(local[8 * q:8 * q + 8], 32 * q, 1)
+    tile = all_sum(tile)
+    lane = lax.broadcasted_iota(jnp.int32, (8, 128), 1)
+    total = [tile] + [pltpu.roll(tile, 128 - 32 * q, 1) for q in range(1, 4)]
+    weights = leaf_weights(jnp.concatenate([jnp.where(lane < 32, part, 0.0) for part in total], axis=0))
+    for r in range(NZ * NX):
+        wbuf[r] = jnp.broadcast_to(weights[r:r + 1], (8, 128))
 
     for k in (4, 3, 5, 2, 6, 1, 7, 0):
         cols = pl.ds(pl.multiple_of(zo(k) * 128, 128), 128)
 
         def combine(g, _, k=k, cols=cols):
             totals = [jnp.zeros((8, 128), jnp.float32)] * 4
-            for r in range(NZ * NX):
-                w = wbuf[r]
+            for r in range(0, NZ * NX, 2):
                 for q in range(4):
-                    rows = pl.ds(pl.multiple_of(g * 32 + 8 * q, 8), 8)
-                    totals[q] = totals[q] + w * leaf[r // 4, r % 4, rows, cols]
+                    both = leaf[g * 4 + q, 8 * r:8 * r + 16, cols].astype(jnp.float32)
+                    totals[q] = totals[q] + wbuf[r] * both[0:8] + wbuf[r + 1] * both[8:16]
             block = jnp.concatenate(totals, axis=0).astype(jnp.bfloat16)
             cst[k, pl.ds(pl.multiple_of(g * 32, 32), 32), :] = block
             return 0
@@ -361,8 +345,8 @@
             pltpu.VMEM((HID, TOK), jnp.bfloat16),
             pltpu.VMEM((NX, NZ, MB, TOK), jnp.bfloat16),
             pltpu.VMEM((NX, NZ, TOK, NB), jnp.bfloat16),
-            pltpu.VMEM((NZ, NX, MB, NB), jnp.float32),
-            pltpu.VMEM((1024, 128), jnp.float32),
+            pltpu.VMEM((MB // 8, 256, NB), jnp.bfloat16),
+            pltpu.VMEM((256, 256), jnp.float32),
             pltpu.VMEM((NZ * NX, 8, 128), jnp.float32),
             pltpu.VMEM((3, 8, 8, 128), jnp.float32),
             pltpu.VMEM((NZ, MB, 128), jnp.bfloat16),

time: 144 us -> 113 us (0.78)
  Pallas kernels: 142 us -> 111 us
    pallas_call x1, Pallas kernels: 142 us -> 111 us  [body(): pl.pallas_call(kernel, out_shape=jax.ShapeDtypeStruct((HID, 128), jnp.bfl...]
where the time goes in v3:
time: 113 us
  Pallas kernels  111 us (98%)
  local copies, waits for them, and re-layouts  1.82 us (2%)
    pallas_call x1, Pallas kernels, body(): pl.pallas_call(kernel, out_shape=jax.ShapeDtypeStruct((HID, 128), jnp.bfl...  111 us

profile of v3, /device:TPU:1, one launch (start us, length us, event | category | flops | bytes accessed | tf_op | source)
XLA Modules:
  0.0 112.5 jit_solution(18069849357350771632)
XLA Ops:
  0.0 110.7 %shard_map.37 = bf16[1792,128]{1,0:T(8,128)(2,1)} custom-call(bf16[256,1792]{1,0:T(8,128)(2,1)} %gate.1, bf16[256,1792]{1,0:T(8,128)(2,1)} %up.1, bf16[256,4096]{1,0:T(8,128)(2,1)} %grad.1), custom_call_target="tpu_custom_call" | custom-call | flops 3760000000 | bytes 5000000 | tf_op jit(solution)/shard_map/pallas_call | solution.py:339
  110.7 1.8 %copy.5 = bf16[1792,128]{1,0:T(8,128)(2,1)} copy(bf16[1792,128]{1,0:T(8,128)(2,1)} %shard_map.37) | data formatting | bytes 917504

commit v4 on v3

--- a/solution.py
+++ b/solution.py
@@ -17,7 +17,7 @@
 TR = TOK // NT
 HR = TOK // 2
 DB = 1024
-GB = 4
+GB = 14
 CS = 768
 ORDER = (0, 7, 1, 6, 2, 5, 3, 4)
 SCHEDULE = (
@@ -338,7 +338,7 @@
     vmem = pl.BlockSpec(memory_space=pltpu.VMEM)
     return pl.pallas_call(
         kernel,
-        out_shape=jax.ShapeDtypeStruct((HID, 128), jnp.bfloat16),
+        out_shape=pltpu.VMEM((HID, 128), jnp.bfloat16),
         in_specs=[vmem, vmem, pl.BlockSpec(memory_space=pl.ANY)],
         out_specs=vmem,
         scratch_shapes=[

time: 113 us -> 110 us (0.973)
  Pallas kernels: 111 us -> 109 us
    pallas_call x1, Pallas kernels: 111 us -> 109 us  [body(): pl.pallas_call(kernel, out_shape=pltpu.VMEM((HID, 128), jnp.bfloat16), in...]
where the time goes in v4:
time: 110 us
  Pallas kernels  109 us (99%)
    pallas_call x1, Pallas kernels, body(): pl.pallas_call(kernel, out_shape=pltpu.VMEM((HID, 128), jnp.bfloat16), in...  109 us

profile of v4, /device:TPU:1, one launch (start us, length us, event | category | flops | bytes accessed | tf_op | source)
XLA Modules:
  0.0 109.7 jit_solution(14339863285061491606)
XLA Ops:
  0.0 108.9 %shard_map.37 = bf16[1792,128]{1,0:T(8,128)(2,1)S(1)} custom-call(bf16[256,1792]{1,0:T(8,128)(2,1)} %gate.1, bf16[256,1792]{1,0:T(8,128)(2,1)} %up.1, bf16[256,4096]{1,0:T(8,128)(2,1)} %grad.1), custom_call_target="tpu_custom_call" | custom-call | flops 3760000000 | bytes 5000000 | tf_op jit(solution)/shard_map/pallas_call | solution.py:339
  109.0 0.8 copy.5

commit v5 on v4

--- a/solution.py
+++ b/solution.py
@@ -16,7 +16,6 @@
 NB = 1024
 TR = TOK // NT
 HR = TOK // 2
-DB = 1024
 GB = 14
 CS = 768
 ORDER = (0, 7, 1, 6, 2, 5, 3, 4)
@@ -111,6 +110,11 @@
         copy.start()
         sent.append(copy)
 
+    def drain(count):
+        for copy in sent[:count]:
+            copy.wait_send()
+        del sent[:count]
+
     def arrived(dst, ss, rs):
         remote(dst, dst, ss, rs, at_x(1)).wait_recv()
 
@@ -248,8 +252,7 @@
             arrived(part, sib_s.at[slot, o], sib_r.at[slot, o])
 
         def product(k, _):
-            xx = 2 * lax.div(k, NB // DB)
-            cols = pl.ds(pl.multiple_of(lax.rem(k, NB // DB) * DB, DB), DB)
+            xx, cols = 2 * k, slice(0, NB)
             first, second = (
                 jnp.dot(hb[xx + m, zc], gb[xx + m, zc, :, cols], preferred_element_type=jnp.float32) for m in range(2)
             )
@@ -259,7 +262,8 @@
                 leaf[g, rows, cols] = both.astype(jnp.bfloat16)
             return 0
 
-        lax.fori_loop(0, 2 * NB // DB, product, 0)
+        for k in range(2):
+            product(k, 0)
 
     def all_sum(value):
         for phase, (count, me) in enumerate(((NT, t), (NX, x), (NZ, z))):
@@ -268,6 +272,7 @@
             for k in range(1, count):
                 where = (at_t(to(k)), at_x(k), at_z(k))[phase]
                 send(slots.at[me], slots.at[me], ar_s.at[phase, k], ar_r.at[phase, k], where)
+            drain(54)
             for k in range(1, count):
                 arrived(slots.at[lax.rem(me + count - k, count)], ar_s.at[phase, k], ar_r.at[phase, k])
             value = jnp.sum(slots[0:count], axis=0)

time: 110 us -> 110 us (level)
  no operation moved by 1% of the time
where the time goes in v5:
time: 110 us; the launch traced here: 109 us
  Pallas kernels  109 us (99%)
    pallas_call x1, Pallas kernels, body(): pl.pallas_call(kernel, out_shape=pltpu.VMEM((HID, 128), jnp.bfloat16), in...  109 us

profile of v5, /device:TPU:1, one launch (start us, length us, event | category | flops | bytes accessed | tf_op | source)
XLA Modules:
  0.0 109.4 jit_solution(1760104145054203785)
XLA Ops:
  0.0 108.6 %shard_map.37 = bf16[1792,128]{1,0:T(8,128)(2,1)S(1)} custom-call(bf16[256,1792]{1,0:T(8,128)(2,1)} %gate.1, bf16[256,1792]{1,0:T(8,128)(2,1)} %up.1, bf16[256,4096]{1,0:T(8,128)(2,1)} %grad.1), custom_call_target="tpu_custom_call" | custom-call | flops 3760000000 | bytes 5000000 | tf_op jit(solution)/shard_map/pallas_call | solution.py:344
  108.6 0.8 copy.5
